TPU v7x, 512 devices: a whole 4x4x16 slice. The times are simulated.
512 devices in a mesh: dp: 16 (over y, z_hi), pipe: 4 (over x), mp: 8 (over z_lo, core).
Axes of the slice: x: 4, y: 4, z: 16 (z_hi: 4, z_lo: 4; z = z_hi * 4 + z_lo), core: 2. Of those that a mesh axis runs over, the one named last changes fastest.
Arguments:
- enc_out: bfloat16 [4096, 4096], P(('dp', 'pipe'), 'mp'), may hold values from -6 to 6
- query: bfloat16 [4, 4096, 4096], P('pipe', 'dp', 'mp'), may hold values from -96 to 96
- w_key: bfloat16 [4, 4096, 4096], P('pipe', 'dp', 'mp'), may hold values from -0.09375 to 0.09375
- w_value: bfloat16 [4, 4096, 4096], P('pipe', 'dp', 'mp'), may hold values from -0.09375 to 0.09375
- d_context: bfloat16 [4, 4096, 4096], P('pipe', 'dp', 'mp'), may hold values from -6 to 6
- enc_lengths: int32 [16], P('dp'), may hold values from 32 to 256
- dec_lengths: int32 [16], P('dp'), may hold values from 32 to 256
Outputs:
- context: bfloat16 [4, 4096, 4096], P('pipe', 'dp', 'mp')
- grad_query: bfloat16 [4, 4096, 4096], P('pipe', 'dp', 'mp')
- grad_enc: float32 [4096, 4096], P(('dp', 'pipe'), 'mp')
All inputs are finite; a program needn't handle non-finite values.
Results may differ from a plain program's by a relative error of at most 0.024.
The roundings to bfloat16 on the way count: a program that leaves them out, or rounds other values in their place, can miss the bound.
Values may be sent and summed in bfloat16 or wider, within the bound.
A program may use at most 64 MiB of HBM per device.

v0:
```python
import jax
import jax.numpy as jnp
from jax import lax
from jax.sharding import PartitionSpec as P

HD = 256


NEG = -1e30


def attend(queries, key_rows, value_rows, cotangent, enc_length, dec_length):
    rows = queries.shape[0]
    length = key_rows.shape[0]
    heads = queries.shape[1] // HD
    scale = HD ** (-0.5)
    query_heads = queries.reshape(rows, heads, HD)
    key_heads = key_rows.reshape(length, heads, HD)
    value_heads = value_rows.reshape(length, heads, HD)
    scores = (
        jnp.einsum("qhd,khd->hqk", query_heads, key_heads, preferred_element_type=jnp.float32)
        * scale
    )
    visible = jnp.arange(length, dtype=jnp.int32) < enc_length
    scores = jnp.where(visible[None, None, :], scores, NEG)
    row_max = jnp.max(scores, axis=2, keepdims=True)
    powers = jnp.exp(scores - row_max)
    attention = powers / jnp.sum(powers, axis=2, keepdims=True)
    rounded = attention.astype(jnp.bfloat16)
    context = jnp.einsum(
        "hqk,khd->qhd", rounded, value_heads, preferred_element_type=jnp.float32
    ).astype(jnp.bfloat16)
    live = (jnp.arange(rows, dtype=jnp.int32) < dec_length)[:, None]
    masked = jnp.where(live, cotangent, jnp.zeros_like(cotangent))
    masked_heads = masked.reshape(rows, heads, HD)
    grad_weights = jnp.einsum(
        "qhd,khd->hqk", masked_heads, value_heads, preferred_element_type=jnp.float32
    )
    row_inner = jnp.sum(masked_heads.astype(jnp.float32) * context.astype(jnp.float32), axis=2)
    grad_scores = (attention * (grad_weights - row_inner.T[:, :, None]) * scale).astype(
        jnp.bfloat16
    )
    grad_query = jnp.einsum(
        "hqk,khd->qhd", grad_scores, key_heads, preferred_element_type=jnp.float32
    )
    grad_key = jnp.einsum(
        "hqk,qhd->khd", grad_scores, query_heads, preferred_element_type=jnp.float32
    )
    grad_value = jnp.einsum(
        "hqk,qhd->khd", rounded, masked_heads, preferred_element_type=jnp.float32
    )
    grad_pair = jnp.stack(
        [grad_key.reshape(length, heads * HD), grad_value.reshape(length, heads * HD)]
    ).astype(jnp.bfloat16)
    return (
        context.reshape(rows, heads * HD),
        grad_query.reshape(rows, heads * HD).astype(jnp.bfloat16),
        grad_pair,
    )


def body(enc_out, query, w_key, w_value, d_context, enc_lengths, dec_lengths):
    wide_rows = lax.all_gather(enc_out, "mp", axis=1, tiled=True)
    enc_full = lax.all_gather(wide_rows, "pipe", axis=0, tiled=True)
    length = enc_full.shape[0]
    width_model = enc_full.shape[1]
    stacked = jnp.stack([w_key[0], w_value[0]])
    weights = lax.all_gather(stacked, "dp", axis=1, tiled=True)
    projected = jnp.einsum("ed,cdh->ceh", enc_full, weights, preferred_element_type=jnp.float32)
    key_rows = projected[0].astype(jnp.bfloat16)
    value_rows = projected[1].astype(jnp.bfloat16)
    context, grad_query, grad_pair = attend(
        query[0], key_rows, value_rows, d_context[0], enc_lengths[0], dec_lengths[0]
    )
    partial_terms = jnp.einsum(
        "ceh,cdh->ed", grad_pair, weights, preferred_element_type=jnp.float32
    )
    section_count = lax.axis_size("pipe")
    model_count = lax.axis_size("mp")
    row_block = length // section_count
    col_block = width_model // model_count
    blocks = partial_terms.reshape(section_count, row_block, model_count, col_block).transpose(
        0, 2, 1, 3
    )
    blocks = blocks.reshape(section_count * model_count * row_block, col_block)
    grad_enc = lax.psum_scatter(blocks, ("pipe", "mp"), scatter_dimension=0, tiled=True)
    return (context[None], grad_query[None], grad_enc)


def solution(mesh):
    in_specs = (
        P(("dp", "pipe"), "mp"),
        P("pipe", "dp", "mp"),
        P("pipe", "dp", "mp"),
        P("pipe", "dp", "mp"),
        P("pipe", "dp", "mp"),
        P("dp"),
        P("dp"),
    )
    out_specs = (P("pipe", "dp", "mp"), P("pipe", "dp", "mp"), P(("dp", "pipe"), "mp"))
    return jax.shard_map(body, mesh=mesh, in_specs=in_specs, out_specs=out_specs, check_vma=False)
```

profile of v0, /device:TPU:24, one launch (start us, length us, event | category | flops | bytes accessed | tf_op | source)
XLA Modules:
  0.0 477.7 jit_solution(4966674270815086640)
XLA Ops:
  7.2 0.0 copy-start
  7.2 0.0 all-gather.5.cloned.1.call-start
  7.2 17.4 %all_gather.10 = bf16[64,4096]{1,0:T(8,128)(2,1)} all-gather(bf16[64,512]{1,0:T(8,128)(2,1)} %param.7), channel_id=1, replica_groups=mesh['dp'=16,'pipe'=4,'mp'=8] {'mp'}, dimensions={1}, use_global_device_ids=true | all-gather | bytes 589824 | tf_op jit(solution)/shard_map/all_gather | solution.py:63
  24.7 0.0 all-gather.5.cloned.1.call-update
  24.7 0.0 all-gather.3.cloned.1.call-start
  24.7 1.1 copy.10
  25.8 1.1 copy.11
  26.9 0.9 pad_maximum_fusion
  27.8 0.0 all-gather.3.cloned.1.call-update
  27.8 0.0 reduce-scatter.2.cloned.1.call-start
  29.1 1.1 copy.39
  30.2 0.0 copy-done
  30.2 0.1 copy.16
  30.4 35.8 %all-gather.5.cloned.1.call-done = bf16[256,4096]{1,0:T(8,128)(2,1)} async-done(((bf16[64,4096]{1,0:T(8,128)(2,1)}), bf16[256,4096]{1,0:T(8,128)(2,1)}) %all-gather.5.cloned.1.call-update) | async-done | bytes 2097168 | tf_op jit(solution)/shard_map/all_gather | solution.py:64
  66.2 232.2 %all-gather.3.cloned.1.call-done = bf16[2,4096,512]{1,2,0:T(8,128)(2,1)} async-done(((bf16[2,256,512]{1,2,0:T(8,128)(2,1)}), bf16[2,4096,512]{1,2,0:T(8,128)(2,1)}) %all-gather.3.cloned.1.call-update) | async-done | bytes 8388624 | tf_op jit(solution)/shard_map/all_gather | solution.py:68
  298.4 6.3 %fusion.7 = bf16[2,256,512]{1,2,0:T(8,128)(2,1)S(1)} fusion(bf16[2,4096,512]{1,2,0:T(8,128)(2,1)} %all-gather.3.cloned.1.call-done, bf16[256,4096]{1,0:T(8,128)(2,1)} %all-gather.5.cloned.1.call-done), kind=kOutput, calls=%fused_computation.6 | convolution fusion | flops 2147745792 | bytes 11010048 | tf_op jit(solution)/shard_map/ed,cdh->ceh/dot_general | solution.py:69
  304.8 0.4 fusion.29
  305.2 0.6 convolution_convert_fusion
  305.8 0.1 copy.25
  306.0 0.6 multiply_reduce_fusion
  306.6 0.3 fusion.15
  306.9 0.3 convolution_convert_fusion.1
  307.2 0.1 copy.24
  307.3 5.7 %fusion.16 = f32[256,4096,1]{1,0,2:T(8,128)S(1)} fusion(bf16[2,4096,512]{1,2,0:T(8,128)(2,1)} %all-gather.3.cloned.1.call-done, bf16[1,256,512]{2,1,0:T(8,128)(2,1)S(1)} %copy.25, bf16[1,256,512]{2,1,0:T(8,128)(2,1)S(1)} %copy.24), kind=kOutput, calls=%fused_computation.20 | convolution fusion | flops 2147745792 | bytes 13107200 | tf_op jit(solution)/shard_map/ceh,cdh->ed/dot_general | solution.py:75
  313.0 3.8 copy.40
  316.8 0.4 bitcast_bitcast_fusion
  317.3 4.4 copy.27
  321.6 0.0 reduce-scatter.2.cloned.1.call-update
  321.7 0.2 convolution_convert_fusion.2
  321.9 0.8 copy.29
  322.7 0.8 copy.28
  323.6 147.6 %reduce-scatter.2.cloned.1.call-done = f32[64,512]{1,0:T(8,128)} async-done(((f32[2048,512]{1,0:T(8,128)}), f32[64,512]{1,0:T(8,128)}) %reduce-scatter.2.cloned.1.call-update) | async-done | bytes 131088 | tf_op jit(solution)/shard_map/reduce_scatter | solution.py:86
  (2 shorter events, 0.0 us)
Async XLA Ops:
  7.2 23.1 %copy-start = (bf16[1,256,512]{2,1,0:T(8,128)(2,1)S(1)}, bf16[1,256,512]{2,1,0:T(8,128)(2,1)}, u32[]{:S(2)}) copy-start(bf16[1,256,512]{2,1,0:T(8,128)(2,1)} %param.11) | copy-start | bytes 786436
  7.2 59.0 %all-gather.5.cloned.1.call-start = ((), (), s32[]{:S(2)}) async-start(), calls=%async_computation.2 | async-start | bytes 2621440 | tf_op jit(solution)/shard_map/all_gather | solution.py:64
  24.7 273.7 %all-gather.3.cloned.1.call-start = ((), (), s32[]{:S(2)}) async-start(), calls=%async_computation.1 | async-start | bytes 8912896 | tf_op jit(solution)/shard_map/all_gather | solution.py:68
  27.8 443.4 %reduce-scatter.2.cloned.1.call-start = ((), (), s32[]{:S(2)}) async-start(), calls=%async_computation.3 | async-start | bytes 4325376 | tf_op jit(solution)/shard_map/reduce_scatter | solution.py:86
Sparse Core Ops, SparseCore 0:
  24.8 41.3 all-gather.4
  69.2 229.1 all-gather.2
  321.8 149.3 reduce-scatter.1
where the time goes:
time: 478 us
  waiting for transfers between devices  416 us (87%)
  blocking collectives  17.4 us (4%)
  between operations  15.2 us (3%)
  matrix products  14.5 us (3%)
  local copies, waits for them, and re-layouts  14 us (3%)
    all_gather x1, waiting for transfers between devices, body(): weights = lax.all_gather(stacked, 'dp', axis=1, tiled=True)  232 us
    reduce_scatter x1, waiting for transfers between devices, body(): lax.psum_scatter(blocks, ('pipe', 'mp'), scatter_dimension=0, tiled=True)  148 us
    all_gather x1, waiting for transfers between devices, body(): enc_full = lax.all_gather(wide_rows, 'pipe', axis=0, tiled=True)  35.8 us
    all_gather x1, blocking collectives, body(): wide_rows = lax.all_gather(enc_out, 'mp', axis=1, tiled=True)  17.4 us
  transfers between devices with their start and end apart: 3, of which 3 were waited for; matrix products, arithmetic and copies ran while one was open for 1% of the time, Pallas kernels for 0%

commit v1 on v0

v1 whole, which is shorter than its diff:
```python
import jax
import jax.numpy as jnp
from jax import lax
from jax.experimental import pallas as pl
from jax.experimental.pallas import tpu as pltpu
from jax.sharding import PartitionSpec as P

HD = 256
NEG = -1e30
BF = jnp.bfloat16
F32 = jnp.float32
CUTS = 4
ROWS = 256 // CUTS
STEPS = 4 * CUTS

NT = (((1,), (1,)), ((), ()))
NN = (((1,), (0,)), ((), ()))
TN = (((0,), (0,)), ((), ()))


def dot(a, b, dims):
    return lax.dot_general(a, b, dims, preferred_element_type=F32)


def kernel(
    enc_len, dec_len, enc_ref, q_ref, wk_ref, wv_ref, dc_ref,
    ctx_ref, gq_ref, ge_ref,
    w, e, acc, kv, grads, s0, r0, part, x1s, x1r, x2s, x2r, zs, zr,
    ez_s, ez_r, ex_s, ex_r, ec_s, ec_r, z_s, z_r, y_s, y_r,
    c_s, c_r, x1_s, x1_r, x2_s, x2_r, q_s, q_r,
):
    dp, x, mp = lax.axis_index("dp"), lax.axis_index("pipe"), lax.axis_index("mp")
    y, zh = dp // 4, dp % 4
    zl, core = mp // 2, mp % 2
    up, down = ((y + 1) % 4) * 4 + zh, ((y + 3) % 4) * 4 + zh
    nxt, prv = y * 4 + (zh + 1) % 4, y * 4 + (zh + 3) % 4
    d_up, d_down = (up, x, mp), (down, x, mp)
    d_next, d_prev = (nxt, x, mp), (prv, x, mp)
    d_right, d_left = (dp, (x + 1) % 4, mp), (dp, (x + 3) % 4, mp)
    d_sib = (dp, x, zl * 2 + 1 - core)
    d_line = [(dp, x, ((zl + r) % 4) * 2 + core) for r in range(4)]

    def rc(src, dst, ssem, rsem, dev):
        return pltpu.make_async_remote_copy(
            src_ref=src, dst_ref=dst, send_sem=ssem, recv_sem=rsem,
            device_id=dev, device_id_type=pl.DeviceIdType.MESH,
        )

    barrier = pltpu.get_barrier_semaphore()
    partners = [d_up, d_down, d_next, d_prev, d_right, d_left, d_sib] + d_line[1:]
    for dev in partners:
        pl.semaphore_signal(barrier, inc=1, device_id=dev, device_id_type=pl.DeviceIdType.MESH)

    w[dp, 0] = wk_ref[0]
    w[dp, 1] = wv_ref[0]
    my_rows = pl.ds(pl.multiple_of(x * 64, 64), 64)
    e[2 * mp, my_rows, :] = enc_ref[:, :256]
    e[2 * mp + 1, my_rows, :] = enc_ref[:, 256:]
    pl.semaphore_wait(barrier, len(partners))

    def eblock(xx, zz, cc):
        return e.at[pl.ds(zz * 4 + cc * 2, 2), pl.ds(pl.multiple_of(xx * 64, 64), 64), :]

    def ehalf(xx, zz, cc, part_of):
        return e.at[zz * 4 + cc * 2 + part_of, pl.ds(pl.multiple_of(xx * 64, 64), 64), :]

    def e_line(r):
        b = eblock(x, zl, core)
        return rc(b, b, ez_s.at[r], ez_r.at[r], d_line[r])

    def e_line_in(r):
        b = eblock(x, (zl + 4 - r) % 4, core)
        return rc(b, b, ez_s.at[r], ez_r.at[r], d_line[r])

    for r in (2, 1, 3):
        e_line(r).start()

    def chunk(yy, zz, j, sub):
        start = pl.multiple_of(sub * ROWS, ROWS)
        return w.at[yy * 4 + zz, j, pl.ds(start, ROWS), :]

    def z_copy(t, forwarded, inbound):
        out = []
        for stream in (0, 1):
            if forwarded:
                j, sub = stream, t - 2 * CUTS
                away = 1 + inbound
            else:
                j = (t // CUTS + stream) % 2
                sub = t % CUTS
                away = inbound
            zz = (zh + 4 - away) % 4 if stream == 0 else (zh + away) % 4
            c = chunk(y, zz, j, sub)
            out.append(rc(c, c, z_s.at[stream, t], z_r.at[stream, t], d_next if stream == 0 else d_prev))
        return out

    def unit(i):
        p, sub = i // CUTS, i % CUTS
        kz = (zh + 3 * p + 3 * (p // 2) + 2 * (p // 3)) % 4
        vz = (zh + p + p // 2 + 2 * (p // 3)) % 4
        return (kz, vz), sub

    def y_direct(i, inbound):
        zz, sub = unit(i)
        out = []
        for j in (0, 1):
            for way in (0, 1):
                yy = y if not inbound else ((y + 3) % 4 if way == 0 else (y + 1) % 4)
                c = chunk(yy, zz[j], j, sub)
                n = j * 2 + way
                out.append(rc(c, c, y_s.at[n, i], y_r.at[n, i], d_up if way == 0 else d_down))
        return out

    def y_forward(i, inbound):
        zz, sub = unit(i)
        out = []
        for j in (0, 1):
            away = 1 + inbound
            yy = (y + 4 - away) % 4 if j == 0 else (y + away) % 4
            c = chunk(yy, zz[j], j, sub)
            out.append(rc(c, c, y_s.at[4 + j, i], y_r.at[4 + j, i], d_up if j == 0 else d_down))
        return out

    def start(copies):
        for c in copies:
            c.start()

    def received(copies):
        for c in copies:
            c.wait_recv()

    def sent(copies):
        for c in copies:
            c.wait_send()

    def loop(lo, hi, body):
        lax.fori_loop(lo, hi, lambda i, carry: (body(i), carry)[1], 0)

    def first(i):
        start(z_copy(i, False, 0))
        start(y_direct(i, 0))

    loop(0, CUTS, first)
    loop(CUTS, 2 * CUTS, lambda i: start(z_copy(i, False, 0)))

    def ex_direct(r, inbound):
        zz = (zl + 4 - r) % 4
        out = []
        for way in (0, 1):
            xx = x if not inbound else ((x + 3) % 4 if way == 0 else (x + 1) % 4)
            b = eblock(xx, zz, core)
            out.append(rc(b, b, ex_s.at[way, r], ex_r.at[way, r], d_right if way == 0 else d_left))
        return out

    def ex_forward(r, inbound):
        zz = (zl + 4 - r) % 4
        out = []
        for way in (0, 1):
            away = 1 + inbound
            xx = (x + 4 - away) % 4 if way == 0 else (x + away) % 4
            b = ehalf(xx, zz, core, way)
            out.append(rc(b, b, ex_s.at[2 + way, r], ex_r.at[2 + way, r], d_right if way == 0 else d_left))
        return out

    def ec_copy(r, inbound):
        cc = 1 - core if inbound else core
        b = e.at[pl.ds(((zl + 4 - r) % 4) * 4 + cc * 2, 2)]
        return rc(b, b, ec_s.at[r], ec_r.at[r], d_sib)

    start(ex_direct(0, 0))
    for r in (1, 3, 2):
        e_line_in(r).wait_recv()
        start(ex_direct(r, 0))
    for r in (0, 1, 3, 2):
        received(ex_direct(r, 1))
        start(ex_forward(r, 0))
    for r in (0, 1, 3, 2):
        received(ex_forward(r, 1))
        ec_copy(r, 0).start()

    def own_phase(i):
        received(y_direct(i, 1))
        start(y_forward(i, 0))

    loop(0, CUTS, own_phase)
    for r in (0, 1, 3, 2):
        ec_copy(r, 1).wait_recv()

    def add_block(yy, zz, begin=False):
        d = yy * 4 + zz
        rows = e[d]
        for j in (0, 1):
            term = dot(rows, w[d, j], NN)
            acc[j] = term if begin else acc[j] + term

    def z_last(i):
        t = i - CUTS
        received(z_copy(t, True, 1))
        start(y_direct(i, 0))
        received(y_direct(i - 1, 1))
        start(y_forward(i - 1, 0))
        received(y_forward(i - 2, 1))

    loop(0, CUTS, lambda i: received(y_forward(i, 1)))
    add_block(y, zh, True)
    loop(1, 4, lambda k: add_block((y + k) % 4, zh))

    def phase_one(i):
        t = i - CUTS
        received(z_copy(t, False, 1))
        start(z_copy(t + 2 * CUTS, True, 0))
        start(y_direct(i, 0))

        @pl.when(t >= 1)
        def _():
            received(y_direct(i - 1, 1))
            start(y_forward(i - 1, 0))

        @pl.when(t >= 2)
        def _():
            received(y_forward(i - 2, 1))

    def phase_two(i):
        received(z_copy(i - CUTS, False, 1))
        start(y_direct(i, 0))
        received(y_direct(i - 1, 1))
        start(y_forward(i - 1, 0))
        received(y_forward(i - 2, 1))

    loop(CUTS, 2 * CUTS, phase_one)
    loop(2 * CUTS, 3 * CUTS, phase_two)
    loop(3 * CUTS, 3 * CUTS + 2, z_last)

    def neighbours(k):
        add_block((y + k) % 4, (zh + 1) % 4)
        add_block((y + k) % 4, (zh + 3) % 4)

    loop(0, 4, neighbours)
    loop(3 * CUTS + 2, 4 * CUTS, z_last)
    received(y_direct(STEPS - 1, 1))
    start(y_forward(STEPS - 1, 0))
    received(y_forward(STEPS - 2, 1))
    far = (zh + 2) % 4
    add_block(y, far)
    add_block((y + 1) % 4, far)
    add_block((y + 3) % 4, far)
    received(y_forward(STEPS - 1, 1))
    add_block((y + 2) % 4, far)

    scale = HD ** -0.5
    kv[...] = acc[...].astype(BF)
    shape = (256, 256)
    visible = lax.broadcasted_iota(jnp.int32, shape, 1) < enc_len[0]
    live = lax.broadcasted_iota(jnp.int32, shape, 0) < dec_len[0]
    for h in (0, 1):
        cols = slice(h * HD, (h + 1) * HD)
        q = q_ref[0, :, cols]
        key, value = kv[0, :, cols], kv[1, :, cols]
        masked = jnp.where(live, dc_ref[0, :, cols].astype(F32), 0.0)
        masked16 = masked.astype(BF)
        scores = jnp.where(visible, dot(q, key, NT) * scale, NEG)
        powers = jnp.exp(scores - jnp.max(scores, axis=1, keepdims=True))
        attention = powers / jnp.sum(powers, axis=1, keepdims=True)
        rounded = attention.astype(BF)
        context = dot(rounded, value, NN).astype(BF)
        ctx_ref[0, :, cols] = context
        weights = dot(masked16, value, NT)
        inner = jnp.sum(masked * context.astype(F32), axis=1, keepdims=True)
        g = (attention * (weights - inner) * scale).astype(BF)
        gq_ref[0, :, cols] = dot(g, key, NN).astype(BF)
        grads[0, :, cols] = dot(g, q, TN).astype(BF)
        grads[1, :, cols] = dot(rounded, masked16, TN).astype(BF)

    def place(k):
        return (zl + 1 + k) % 4

    def enc_term(k, cc, half):
        d = place(k) * 4 + cc * 2 + half
        return dot(grads[0], w[d, 0], NT) + dot(grads[1], w[d, 1], NT)

    def c_copy(k):
        return rc(s0.at[k], r0.at[k], c_s.at[k], c_r.at[k], d_sib)

    def quarter(n):
        return pl.ds(pl.multiple_of(((x + n) % 4) * 64, 64), 64)

    def x1_copy(k):
        return [
            rc(x1s.at[k, way], x1r.at[k, way], x1_s.at[k, way], x1_r.at[k, way], dev)
            for way, dev in ((0, d_right), (1, d_left))
        ]

    def x2_copy(k):
        return [
            rc(x2s.at[k, way], x2r.at[k, way], x2_s.at[k, way], x2_r.at[k, way], dev)
            for way, dev in ((0, d_right), (1, d_left))
        ]

    def q_copy(k):
        return rc(zs.at[k], zr.at[k], q_s.at[k], q_r.at[k], d_line[k + 1])

    def to_sibling(k):
        for half in (0, 1):
            s0[k, half] = enc_term(k, 1 - core, half).astype(BF)
        c_copy(k).start()

    def mine(k):
        for half in (0, 1):
            part[k, half] = enc_term(k, core, half)
        c_copy(k).wait_recv()
        part[k] = part[k] + r0[k].astype(F32)
        for way in (0, 1):
            x1s[k, way] = part[k, way, quarter(2), :].astype(BF)
        start(x1_copy(k))

    def second(k):
        received(x1_copy(k))
        for way in (0, 1):
            away = quarter(1 + 2 * way)
            for half in (0, 1):
                term = part[k, half, away, :]
                if half == way:
                    term = term + x1r[k, way].astype(F32)
                x2s[k, way, half] = term.astype(BF)
        start(x2_copy(k))

    def third(k):
        received(x2_copy(k))
        total = part[k, :, quarter(0), :] + x2r[k, 0].astype(F32) + x2r[k, 1].astype(F32)
        part[k, :, quarter(0), :] = total

    loop(0, 4, to_sibling)
    loop(0, 4, mine)
    loop(0, 4, second)
    for k in range(3):
        third(k)
        zs[k] = part[k, :, quarter(0), :].astype(BF)
        q_copy(k).start()
    third(3)
    total = part[3, :, quarter(0), :]
    for k in range(3):
        q_copy(k).wait_recv()
        total = total + zr[k].astype(F32)
    ge_ref[:, :256] = total[0]
    ge_ref[:, 256:] = total[1]

    for r in range(1, 4):
        e_line(r).wait_send()
    for r in range(4):
        sent(ex_direct(r, 0))
        sent(ex_forward(r, 0))
        ec_copy(r, 0).wait_send()
    loop(0, 2 * CUTS, lambda t: sent(z_copy(t, False, 0)))
    loop(2 * CUTS, 3 * CUTS, lambda t: sent(z_copy(t, True, 0)))

    def y_sent(i):
        sent(y_direct(i, 0))
        sent(y_forward(i, 0))

    loop(0, STEPS, y_sent)

    def rest(k):
        c_copy(k).wait_send()
        sent(x1_copy(k))
        sent(x2_copy(k))

    loop(0, 4, rest)
    for k in range(3):
        q_copy(k).wait_send()


def body(enc_out, query, w_key, w_value, d_context, enc_lengths, dec_lengths):
    vmem = pl.BlockSpec(memory_space=pltpu.VMEM)
    smem = pl.BlockSpec(memory_space=pltpu.SMEM)
    dma = pltpu.SemaphoreType.DMA
    return pl.pallas_call(
        kernel,
        out_shape=(
            jax.ShapeDtypeStruct((1, 256, 512), BF),
            jax.ShapeDtypeStruct((1, 256, 512), BF),
            jax.ShapeDtypeStruct((64, 512), F32),
        ),
        in_specs=[smem, smem] + [vmem] * 5,
        out_specs=(vmem, vmem, vmem),
        scratch_shapes=[
            pltpu.VMEM((16, 2, 256, 512), BF),
            pltpu.VMEM((16, 256, 256), BF),
            pltpu.VMEM((2, 256, 512), F32),
            pltpu.VMEM((2, 256, 512), BF),
            pltpu.VMEM((2, 256, 512), BF),
            pltpu.VMEM((4, 2, 256, 256), BF),
            pltpu.VMEM((4, 2, 256, 256), BF),
            pltpu.VMEM((4, 2, 256, 256), F32),
            pltpu.VMEM((4, 2, 64, 256), BF),
            pltpu.VMEM((4, 2, 64, 256), BF),
            pltpu.VMEM((4, 2, 2, 64, 256), BF),
            pltpu.VMEM((4, 2, 2, 64, 256), BF),
            pltpu.VMEM((3, 2, 64, 256), BF),
            pltpu.VMEM((3, 2, 64, 256), BF),
            dma((4,)), dma((4,)),
            dma((4, 4)), dma((4, 4)),
            dma((4,)), dma((4,)),
            dma((2, 3 * CUTS)), dma((2, 3 * CUTS)),
            dma((6, STEPS)), dma((6, STEPS)),
            dma((4,)), dma((4,)),
            dma((4, 2)), dma((4, 2)),
            dma((4, 2)), dma((4, 2)),
            dma((3,)), dma((3,)),
        ],
        compiler_params=pltpu.CompilerParams(
            collective_id=0, has_side_effects=True, vmem_limit_bytes=48 * 1024 * 1024
        ),
        cost_estimate=pl.CostEstimate(flops=5 * 10**9, bytes_accessed=2 * 10**6, transcendentals=131072),
        name="fused",
    )(enc_lengths, dec_lengths, enc_out, query, w_key, w_value, d_context)


def solution(mesh):
    in_specs = (
        P(("dp", "pipe"), "mp"),
        P("pipe", "dp", "mp"),
        P("pipe", "dp", "mp"),
        P("pipe", "dp", "mp"),
        P("pipe", "dp", "mp"),
        P("dp"),
        P("dp"),
    )
    out_specs = (P("pipe", "dp", "mp"), P("pipe", "dp", "mp"), P(("dp", "pipe"), "mp"))
    return jax.shard_map(body, mesh=mesh, in_specs=in_specs, out_specs=out_specs, check_vma=False)
```

time: 478 us -> 152 us (0.32)
  waiting for transfers between devices: 416 us -> 0 us
  Pallas kernels: 0 us -> 143 us
  blocking collectives: 17.4 us -> 0 us
  matrix products: 14.5 us -> 0 us
  between operations: 15.2 us -> 1.95 us
  local copies, waits for them, and re-layouts: 14 us -> 6.69 us
    all_gather x2 -> x0, waiting for transfers between devices: 268 us -> none  [the longest x1 232 us: body(): weights = lax.all_gather(stacked, 'dp', axis=1, tiled=True)]
    reduce_scatter x1 -> x0, waiting for transfers between devices: 148 us -> none  [body(): lax.psum_scatter(blocks, ('pipe', 'mp'), scatter_dimension=0, tiled=True)]
    pallas_call x0 -> x1, Pallas kernels: none -> 143 us  [body(): pl.pallas_call(kernel, out_shape=(jax.ShapeDtypeStruct((1, 256, 512), BF)...]
    all_gather x1 -> x0, blocking collectives: 17.4 us -> none  [body(): wide_rows = lax.all_gather(enc_out, 'mp', axis=1, tiled=True)]
    dot_general x7 -> x0, matrix products: 14.1 us -> none  [the longest x1 6.35 us: body(): jnp.einsum('ed,cdh->ceh', enc_full, weights, preferred_element_type=jnp.f...]
    transpose x2 -> x0, local copies, waits for them, and re-layouts: 4.8 us -> none  [body(): partial_terms.reshape(section_count, row_block, model_count, col_block)]
  transfers between devices with their start and end apart: 3 -> 0, of which waited for: 3 -> 0; matrix products, arithmetic and copies ran while one was open for 1% -> 0% of each run, Pallas kernels for 0% -> 0%
where the time goes in v1:
time: 152 us; the launch traced here: 151 us
  Pallas kernels  143 us (94%)
  local copies, waits for them, and re-layouts  6.69 us (4%)
  between operations  1.95 us (1%)
    pallas_call x1, Pallas kernels, body(): pl.pallas_call(kernel, out_shape=(jax.ShapeDtypeStruct((1, 256, 512), BF)...  143 us
    unnamed x13, local copies, waits for them, and re-layouts  6.69 us

profile of v1, /device:TPU:24, one launch (start us, length us, event | category | flops | bytes accessed | tf_op | source)
XLA Modules:
  0.0 151.4 jit_solution(17965278028164473636)
XLA Ops:
  1.9 0.0 copy-start
  1.9 0.9 copy-done
  2.9 0.0 copy-start.1
  2.9 0.9 copy-done.1
  3.8 0.0 copy-start.2
  3.8 0.9 copy-done.2
  4.8 0.0 copy-start.3
  4.8 0.9 copy-done.3
  5.7 0.0 copy-start.4
  5.7 0.8 copy-done.4
  6.6 142.8 %fused.1 = (bf16[1,256,512]{2,1,0:T(8,128)(2,1)S(1)}, bf16[1,256,512]{2,1,0:T(8,128)(2,1)S(1)}, f32[64,512]{1,0:T(8,128)S(1)}) custom-call(s32[1]{0:T(128)S(6)} %copy.13.enc_len, s32[1]{0:T(128)S(6)} %copy.14.dec_len, bf16[64,512]{1,0:T(8,128)(2,1)S(1)} %copy-done.4, bf16[1,256,512]{2,1,0:T(8,128)(2,1)S(1)} %copy-done, bf16[1,256,512]{2,1,0:T(8,128)(2,1)S(1)} %copy-done.1, ...), custom_call_target="tpu_custom_call" | custom-call | flops 5000000000 | bytes 2000000 | tf_op jit(solution)/shard_map/fused/pallas_call | solution.py:376
  149.4 0.7 copy.15
  150.1 0.7 copy.16
  150.8 0.7 copy.17
Async XLA Ops:
  1.9 1.0 copy-start
  2.9 0.9 copy-start.1
  3.8 0.9 copy-start.2
  4.8 0.9 copy-start.3
  5.7 0.8 copy-start.4

commit v2 on v1

--- a/solution.py
+++ b/solution.py
@@ -9,9 +9,21 @@
 NEG = -1e30
 BF = jnp.bfloat16
 F32 = jnp.float32
-CUTS = 4
-ROWS = 256 // CUTS
-STEPS = 4 * CUTS
+FIRST = (16, 32, 48, 64, 64, 32)
+SECOND = (64, 64, 64, 64)
+THIRD = (64, 64, 48, 32, 32, 16)
+OWN = (64, 64, 64, 64)
+DEPTH = 4
+LAG = 1
+
+
+def spans(stage, sizes):
+    return [(stage, sum(sizes[:n]), size) for n, size in enumerate(sizes)]
+
+
+Z = spans(0, FIRST) + spans(1, SECOND) + spans(2, THIRD)
+UNITS = spans(-1, OWN) + Z
+NZ, NO, NU = len(Z), len(OWN), len(UNITS)
 
 NT = (((1,), (1,)), ((), ()))
 NN = (((1,), (0,)), ((), ()))
@@ -27,7 +39,7 @@
     ctx_ref, gq_ref, ge_ref,
     w, e, acc, kv, grads, s0, r0, part, x1s, x1r, x2s, x2r, zs, zr,
     ez_s, ez_r, ex_s, ex_r, ec_s, ec_r, z_s, z_r, y_s, y_r,
-    c_s, c_r, x1_s, x1_r, x2_s, x2_r, q_s, q_r,
+    c_s, c_r, x1_s, x1_r, x2_s, x2_r, q_s, q_r, in_s, q_v, dc_v,
 ):
     dp, x, mp = lax.axis_index("dp"), lax.axis_index("pipe"), lax.axis_index("mp")
     y, zh = dp // 4, dp % 4
@@ -51,11 +63,20 @@
     for dev in partners:
         pl.semaphore_signal(barrier, inc=1, device_id=dev, device_id_type=pl.DeviceIdType.MESH)
 
-    w[dp, 0] = wk_ref[0]
-    w[dp, 1] = wv_ref[0]
     my_rows = pl.ds(pl.multiple_of(x * 64, 64), 64)
-    e[2 * mp, my_rows, :] = enc_ref[:, :256]
-    e[2 * mp + 1, my_rows, :] = enc_ref[:, 256:]
+    loads = [
+        pltpu.make_async_copy(wk_ref.at[0], w.at[dp, 0], in_s.at[0]),
+        pltpu.make_async_copy(wv_ref.at[0], w.at[dp, 1], in_s.at[1]),
+        pltpu.make_async_copy(enc_ref.at[:, pl.ds(0, 256)], e.at[2 * mp, my_rows, :], in_s.at[2]),
+        pltpu.make_async_copy(enc_ref.at[:, pl.ds(256, 256)], e.at[2 * mp + 1, my_rows, :], in_s.at[3]),
+        pltpu.make_async_copy(q_ref.at[0], q_v, in_s.at[4]),
+        pltpu.make_async_copy(dc_ref.at[0], dc_v, in_s.at[5]),
+    ]
+    for copy in loads:
+        copy.start()
+    acc[...] = jnp.zeros_like(acc)
+    for copy in loads[:4]:
+        copy.wait()
     pl.semaphore_wait(barrier, len(partners))
 
     def eblock(xx, zz, cc):
@@ -72,52 +93,39 @@
         b = eblock(x, (zl + 4 - r) % 4, core)
         return rc(b, b, ez_s.at[r], ez_r.at[r], d_line[r])
 
-    for r in (2, 1, 3):
-        e_line(r).start()
-
-    def chunk(yy, zz, j, sub):
-        start = pl.multiple_of(sub * ROWS, ROWS)
-        return w.at[yy * 4 + zz, j, pl.ds(start, ROWS), :]
-
-    def z_copy(t, forwarded, inbound):
+    def chunk(yy, zz, j, first, rows):
+        return w.at[yy * 4 + zz, j, pl.ds(first, rows), :]
+
+    def z_copy(t, inbound):
+        stage, first, rows = Z[t]
+        away = stage // 2 + inbound
         out = []
         for stream in (0, 1):
-            if forwarded:
-                j, sub = stream, t - 2 * CUTS
-                away = 1 + inbound
-            else:
-                j = (t // CUTS + stream) % 2
-                sub = t % CUTS
-                away = inbound
             zz = (zh + 4 - away) % 4 if stream == 0 else (zh + away) % 4
-            c = chunk(y, zz, j, sub)
+            c = chunk(y, zz, (stage + stream) % 2, first, rows)
             out.append(rc(c, c, z_s.at[stream, t], z_r.at[stream, t], d_next if stream == 0 else d_prev))
         return out
 
-    def unit(i):
-        p, sub = i // CUTS, i % CUTS
-        kz = (zh + 3 * p + 3 * (p // 2) + 2 * (p // 3)) % 4
-        vz = (zh + p + p // 2 + 2 * (p // 3)) % 4
-        return (kz, vz), sub
-
     def y_direct(i, inbound):
-        zz, sub = unit(i)
+        stage, first, rows = UNITS[i]
+        zz = [(zh + n) % 4 for n in ((0, 0), (3, 1), (1, 3), (2, 2))[stage + 1]]
         out = []
         for j in (0, 1):
             for way in (0, 1):
                 yy = y if not inbound else ((y + 3) % 4 if way == 0 else (y + 1) % 4)
-                c = chunk(yy, zz[j], j, sub)
+                c = chunk(yy, zz[j], j, first, rows)
                 n = j * 2 + way
                 out.append(rc(c, c, y_s.at[n, i], y_r.at[n, i], d_up if way == 0 else d_down))
         return out
 
     def y_forward(i, inbound):
-        zz, sub = unit(i)
+        stage, first, rows = UNITS[i]
+        zz = [(zh + n) % 4 for n in ((0, 0), (3, 1), (1, 3), (2, 2))[stage + 1]]
         out = []
         for j in (0, 1):
             away = 1 + inbound
             yy = (y + 4 - away) % 4 if j == 0 else (y + away) % 4
-            c = chunk(yy, zz[j], j, sub)
+            c = chunk(yy, zz[j], j, first, rows)
             out.append(rc(c, c, y_s.at[4 + j, i], y_r.at[4 + j, i], d_up if j == 0 else d_down))
         return out
 
@@ -135,13 +143,6 @@
 
     def loop(lo, hi, body):
         lax.fori_loop(lo, hi, lambda i, carry: (body(i), carry)[1], 0)
-
-    def first(i):
-        start(z_copy(i, False, 0))
-        start(y_direct(i, 0))
-
-    loop(0, CUTS, first)
-    loop(CUTS, 2 * CUTS, lambda i: start(z_copy(i, False, 0)))
 
     def ex_direct(r, inbound):
         zz = (zl + 4 - r) % 4
@@ -167,86 +168,84 @@
         b = e.at[pl.ds(((zl + 4 - r) % 4) * 4 + cc * 2, 2)]
         return rc(b, b, ec_s.at[r], ec_r.at[r], d_sib)
 
-    start(ex_direct(0, 0))
-    for r in (1, 3, 2):
-        e_line_in(r).wait_recv()
-        start(ex_direct(r, 0))
-    for r in (0, 1, 3, 2):
-        received(ex_direct(r, 1))
-        start(ex_forward(r, 0))
-    for r in (0, 1, 3, 2):
-        received(ex_forward(r, 1))
-        ec_copy(r, 0).start()
-
-    def own_phase(i):
-        received(y_direct(i, 1))
-        start(y_forward(i, 0))
-
-    loop(0, CUTS, own_phase)
-    for r in (0, 1, 3, 2):
-        ec_copy(r, 1).wait_recv()
-
-    def add_block(yy, zz, begin=False):
+    def add_block(yy, zz):
         d = yy * 4 + zz
         rows = e[d]
         for j in (0, 1):
-            term = dot(rows, w[d, j], NN)
-            acc[j] = term if begin else acc[j] + term
-
-    def z_last(i):
-        t = i - CUTS
-        received(z_copy(t, True, 1))
-        start(y_direct(i, 0))
-        received(y_direct(i - 1, 1))
-        start(y_forward(i - 1, 0))
-        received(y_forward(i - 2, 1))
-
-    loop(0, CUTS, lambda i: received(y_forward(i, 1)))
-    add_block(y, zh, True)
-    loop(1, 4, lambda k: add_block((y + k) % 4, zh))
-
-    def phase_one(i):
-        t = i - CUTS
-        received(z_copy(t, False, 1))
-        start(z_copy(t + 2 * CUTS, True, 0))
-        start(y_direct(i, 0))
-
-        @pl.when(t >= 1)
-        def _():
-            received(y_direct(i - 1, 1))
-            start(y_forward(i - 1, 0))
-
-        @pl.when(t >= 2)
-        def _():
-            received(y_forward(i - 2, 1))
-
-    def phase_two(i):
-        received(z_copy(i - CUTS, False, 1))
-        start(y_direct(i, 0))
-        received(y_direct(i - 1, 1))
-        start(y_forward(i - 1, 0))
-        received(y_forward(i - 2, 1))
-
-    loop(CUTS, 2 * CUTS, phase_one)
-    loop(2 * CUTS, 3 * CUTS, phase_two)
-    loop(3 * CUTS, 3 * CUTS + 2, z_last)
+            acc[j] = acc[j] + dot(rows, w[d, j], NN)
+
+    def own(k):
+        add_block((y + k) % 4, zh)
 
     def neighbours(k):
         add_block((y + k) % 4, (zh + 1) % 4)
         add_block((y + k) % 4, (zh + 3) % 4)
 
+    def far(k):
+        add_block((y + k) % 4, (zh + 2) % 4)
+
+    def enc_stage(n):
+        if n == 0:
+            for r in (1, 3, 2):
+                e_line_in(r).wait_recv()
+                start(ex_direct(r, 0))
+        elif n == 1:
+            for r in (0, 1, 3, 2):
+                received(ex_direct(r, 1))
+                start(ex_forward(r, 0))
+        elif n == 2:
+            for r in (0, 1, 3, 2):
+                received(ex_forward(r, 1))
+                ec_copy(r, 0).start()
+        elif n == 3:
+            for r in (0, 1, 3, 2):
+                ec_copy(r, 1).wait_recv()
+
+    for r in (2, 1, 3):
+        e_line(r).start()
+    start(ex_direct(0, 0))
+    for t in range(DEPTH):
+        start(z_copy(t, 0))
+    for i in range(NO):
+        start(y_direct(i, 0))
+    stepped = 0
+
+    def y_until(n):
+        nonlocal stepped
+        while stepped < n:
+            received(y_direct(stepped, 1))
+            start(y_forward(stepped, 0))
+            stepped += 1
+
+    late = 0
+
+    def late_until(n):
+        nonlocal late
+        while late < n:
+            received(y_forward(late, 1))
+            late += 1
+
+    for t in range(NZ):
+        received(z_copy(t, 1))
+        start(y_direct(NO + t, 0))
+        sent(z_copy(t, 0))
+        if t + DEPTH < NZ:
+            start(z_copy(t + DEPTH, 0))
+        y_until(min(NO + t - LAG, (NU * (t + 1)) // NZ))
+        enc_stage(t - 1)
+        if t == 9:
+            late_until(NO)
+            loop(0, 4, own)
+    near = NO + len(FIRST) + len(SECOND)
+    y_until(NU - 1)
+    late_until(near)
     loop(0, 4, neighbours)
-    loop(3 * CUTS + 2, 4 * CUTS, z_last)
-    received(y_direct(STEPS - 1, 1))
-    start(y_forward(STEPS - 1, 0))
-    received(y_forward(STEPS - 2, 1))
-    far = (zh + 2) % 4
-    add_block(y, far)
-    add_block((y + 1) % 4, far)
-    add_block((y + 3) % 4, far)
-    received(y_forward(STEPS - 1, 1))
-    add_block((y + 2) % 4, far)
-
+    y_until(NU)
+    late_until(NU)
+    loop(0, 4, far)
+
+    for copy in loads[4:]:
+        copy.wait()
     scale = HD ** -0.5
     kv[...] = acc[...].astype(BF)
     shape = (256, 256)
@@ -254,9 +253,9 @@
     live = lax.broadcasted_iota(jnp.int32, shape, 0) < dec_len[0]
     for h in (0, 1):
         cols = slice(h * HD, (h + 1) * HD)
-        q = q_ref[0, :, cols]
+        q = q_v[:, cols]
         key, value = kv[0, :, cols], kv[1, :, cols]
-        masked = jnp.where(live, dc_ref[0, :, cols].astype(F32), 0.0)
+        masked = jnp.where(live, dc_v[:, cols].astype(F32), 0.0)
         masked16 = masked.astype(BF)
         scores = jnp.where(visible, dot(q, key, NT) * scale, NEG)
         powers = jnp.exp(scores - jnp.max(scores, axis=1, keepdims=True))
@@ -350,14 +349,10 @@
         sent(ex_direct(r, 0))
         sent(ex_forward(r, 0))
         ec_copy(r, 0).wait_send()
-    loop(0, 2 * CUTS, lambda t: sent(z_copy(t, False, 0)))
-    loop(2 * CUTS, 3 * CUTS, lambda t: sent(z_copy(t, True, 0)))
-
-    def y_sent(i):
+
+    for i in range(NU):
         sent(y_direct(i, 0))
         sent(y_forward(i, 0))
-
-    loop(0, STEPS, y_sent)
 
     def rest(k):
         c_copy(k).wait_send()
@@ -372,6 +367,7 @@
 def body(enc_out, query, w_key, w_value, d_context, enc_lengths, dec_lengths):
     vmem = pl.BlockSpec(memory_space=pltpu.VMEM)
     smem = pl.BlockSpec(memory_space=pltpu.SMEM)
+    hbm = pl.BlockSpec(memory_space=pltpu.HBM)
     dma = pltpu.SemaphoreType.DMA
     return pl.pallas_call(
         kernel,
@@ -380,7 +376,7 @@
             jax.ShapeDtypeStruct((1, 256, 512), BF),
             jax.ShapeDtypeStruct((64, 512), F32),
         ),
-        in_specs=[smem, smem] + [vmem] * 5,
+        in_specs=[smem, smem] + [hbm] * 5,
         out_specs=(vmem, vmem, vmem),
         scratch_shapes=[
             pltpu.VMEM((16, 2, 256, 512), BF),
@@ -400,15 +396,17 @@
             dma((4,)), dma((4,)),
             dma((4, 4)), dma((4, 4)),
             dma((4,)), dma((4,)),
-            dma((2, 3 * CUTS)), dma((2, 3 * CUTS)),
-            dma((6, STEPS)), dma((6, STEPS)),
+            dma((2, NZ)), dma((2, NZ)),
+            dma((6, NU)), dma((6, NU)),
             dma((4,)), dma((4,)),
             dma((4, 2)), dma((4, 2)),
             dma((4, 2)), dma((4, 2)),
-            dma((3,)), dma((3,)),
+            dma((3,)), dma((3,)), dma((6,)),
+            pltpu.VMEM((256, 512), BF),
+            pltpu.VMEM((256, 512), BF),
         ],
         compiler_params=pltpu.CompilerParams(
-            collective_id=0, has_side_effects=True, vmem_limit_bytes=48 * 1024 * 1024
+            collective_id=0, has_side_effects=True, vmem_limit_bytes=64 * 1024 * 1024
         ),
         cost_estimate=pl.CostEstimate(flops=5 * 10**9, bytes_accessed=2 * 10**6, transcendentals=131072),
         name="fused",

time: 152 us -> 142 us (0.934)
  Pallas kernels: 143 us -> 137 us
  local copies, waits for them, and re-layouts: 6.69 us -> 3.37 us
    pallas_call x1, Pallas kernels: 143 us -> 137 us  [body(): pl.pallas_call(kernel, out_shape=(jax.ShapeDtypeStruct((1, 256, 512), BF)...]
    unnamed x13 -> x7, local copies, waits for them, and re-layouts: 6.69 us -> 3.37 us
where the time goes in v2:
time: 142 us
  Pallas kernels  137 us (96%)
  local copies, waits for them, and re-layouts  3.37 us (2%)
  between operations  1.94 us (1%)
    pallas_call x1, Pallas kernels, body(): pl.pallas_call(kernel, out_shape=(jax.ShapeDtypeStruct((1, 256, 512), BF)...  137 us
    unnamed x7, local copies, waits for them, and re-layouts  3.37 us

profile of v2, /device:TPU:24, one launch (start us, length us, event | category | flops | bytes accessed | tf_op | source)
XLA Modules:
  0.0 141.8 jit_solution(13420237121080065778)
XLA Ops:
  1.9 136.5 %fused.1 = (bf16[1,256,512]{2,1,0:T(8,128)(2,1)}, bf16[1,256,512]{2,1,0:T(8,128)(2,1)}, f32[64,512]{1,0:T(8,128)}) custom-call(s32[1]{0:T(128)S(6)} %copy.13.enc_len, s32[1]{0:T(128)S(6)} %copy.14.dec_len, bf16[64,512]{1,0:T(8,128)(2,1)} %enc_ref.1, bf16[1,256,512]{2,1,0:T(8,128)(2,1)} %q_ref.1, bf16[1,256,512]{2,1,0:T(8,128)(2,1)} %wk_ref.1, ...), custom_call_target="tpu_custom_call" | custom-call | flops 5000000000 | bytes 2000000 | tf_op jit(solution)/shard_map/fused/pallas_call | solution.py:372
  138.5 0.0 copy-start
  138.5 1.7 %copy.15 = bf16[1,256,512]{2,1,0:T(8,128)(2,1)} copy(bf16[1,256,512]{2,1,0:T(8,128)(2,1)} %get-tuple-element.6) | data formatting | bytes 524288
  140.2 0.0 copy-done
  140.2 0.0 copy-start.1
  140.2 0.7 copy.16
  140.9 0.3 copy-done.1
  141.2 0.7 copy.17
Async XLA Ops:
  138.5 1.7 %copy-start = (bf16[1,256,512]{2,1,0:T(8,128)(2,1)S(1)}, bf16[1,256,512]{2,1,0:T(8,128)(2,1)}, u32[]{:S(2)}) copy-start(bf16[1,256,512]{2,1,0:T(8,128)(2,1)} %get-tuple-element.7) | copy-start | bytes 786436
  140.2 1.0 copy-start.1

commit v3 on v2

--- a/solution.py
+++ b/solution.py
@@ -9,21 +9,24 @@
 NEG = -1e30
 BF = jnp.bfloat16
 F32 = jnp.float32
-FIRST = (16, 32, 48, 64, 64, 32)
-SECOND = (64, 64, 64, 64)
-THIRD = (64, 64, 48, 32, 32, 16)
-OWN = (64, 64, 64, 64)
-DEPTH = 4
+HEAD0 = ((64,) * 4,) * 3
+HEAD1 = ((64,) * 4,) * 3
+OWN = (128, 128)
+DEPTH = 6
 LAG = 1
-
-
-def spans(stage, sizes):
-    return [(stage, sum(sizes[:n]), size) for n, size in enumerate(sizes)]
-
-
-Z = spans(0, FIRST) + spans(1, SECOND) + spans(2, THIRD)
-UNITS = spans(-1, OWN) + Z
-NZ, NO, NU = len(Z), len(OWN), len(UNITS)
+ENC = (1, 3, 5, 7)
+
+
+def spans(head, stage, sizes):
+    return [(head, stage, sum(sizes[:n]), size) for n, size in enumerate(sizes)]
+
+
+Z = [m for h, sizes in enumerate((HEAD0, HEAD1)) for stage in range(3) for m in spans(h, stage, sizes[stage])]
+UNITS = spans(0, -1, OWN) + spans(1, -1, OWN) + Z
+NZ, NO, NU = len(Z), 2 * len(OWN), 2 * len(OWN) + len(Z)
+NZ0 = sum(len(sizes) for sizes in HEAD0)
+CUT_NEAR = len(HEAD0[0]) + len(HEAD0[1])
+
 
 NT = (((1,), (1,)), ((), ()))
 NN = (((1,), (0,)), ((), ()))
@@ -37,9 +40,9 @@
 def kernel(
     enc_len, dec_len, enc_ref, q_ref, wk_ref, wv_ref, dc_ref,
     ctx_ref, gq_ref, ge_ref,
-    w, e, acc, kv, grads, s0, r0, part, x1s, x1r, x2s, x2r, zs, zr,
+    w, e, acc, grads, away, s0, r0, part, x1s, x1r, x2s, x2r, zs, zr,
     ez_s, ez_r, ex_s, ex_r, ec_s, ec_r, z_s, z_r, y_s, y_r,
-    c_s, c_r, x1_s, x1_r, x2_s, x2_r, q_s, q_r, in_s, q_v, dc_v,
+    c_s, c_r, x1_s, x1_r, x2_s, x2_r, q_s, q_r, in_s, q_v, dc_v, cred,
 ):
     dp, x, mp = lax.axis_index("dp"), lax.axis_index("pipe"), lax.axis_index("mp")
     y, zh = dp // 4, dp % 4
@@ -65,17 +68,19 @@
 
     my_rows = pl.ds(pl.multiple_of(x * 64, 64), 64)
     loads = [
-        pltpu.make_async_copy(wk_ref.at[0], w.at[dp, 0], in_s.at[0]),
-        pltpu.make_async_copy(wv_ref.at[0], w.at[dp, 1], in_s.at[1]),
-        pltpu.make_async_copy(enc_ref.at[:, pl.ds(0, 256)], e.at[2 * mp, my_rows, :], in_s.at[2]),
-        pltpu.make_async_copy(enc_ref.at[:, pl.ds(256, 256)], e.at[2 * mp + 1, my_rows, :], in_s.at[3]),
-        pltpu.make_async_copy(q_ref.at[0], q_v, in_s.at[4]),
-        pltpu.make_async_copy(dc_ref.at[0], dc_v, in_s.at[5]),
+        pltpu.make_async_copy(ref.at[0, :, pl.ds(h * HD, HD)], w.at[dp, h, j], in_s.at[4 + 2 * h + j])
+        for h in (0, 1)
+        for j, ref in ((0, wk_ref), (1, wv_ref))
+    ] + [
+        pltpu.make_async_copy(enc_ref.at[:, pl.ds(0, 256)], e.at[2 * mp, my_rows, :], in_s.at[0]),
+        pltpu.make_async_copy(enc_ref.at[:, pl.ds(256, 256)], e.at[2 * mp + 1, my_rows, :], in_s.at[1]),
+        pltpu.make_async_copy(q_ref.at[0], q_v, in_s.at[2]),
+        pltpu.make_async_copy(dc_ref.at[0], dc_v, in_s.at[3]),
     ]
     for copy in loads:
         copy.start()
     acc[...] = jnp.zeros_like(acc)
-    for copy in loads[:4]:
+    for copy in loads[:6]:
         copy.wait()
     pl.semaphore_wait(barrier, len(partners))
 
@@ -93,39 +98,39 @@
         b = eblock(x, (zl + 4 - r) % 4, core)
         return rc(b, b, ez_s.at[r], ez_r.at[r], d_line[r])
 
-    def chunk(yy, zz, j, first, rows):
-        return w.at[yy * 4 + zz, j, pl.ds(first, rows), :]
+    def chunk(yy, zz, h, j, first, rows):
+        return w.at[yy * 4 + zz, h, j, pl.ds(first, rows), :]
 
     def z_copy(t, inbound):
-        stage, first, rows = Z[t]
+        h, stage, first, rows = Z[t]
         away = stage // 2 + inbound
         out = []
         for stream in (0, 1):
             zz = (zh + 4 - away) % 4 if stream == 0 else (zh + away) % 4
-            c = chunk(y, zz, (stage + stream) % 2, first, rows)
+            c = chunk(y, zz, h, (stage + stream) % 2, first, rows)
             out.append(rc(c, c, z_s.at[stream, t], z_r.at[stream, t], d_next if stream == 0 else d_prev))
         return out
 
     def y_direct(i, inbound):
-        stage, first, rows = UNITS[i]
+        h, stage, first, rows = UNITS[i]
         zz = [(zh + n) % 4 for n in ((0, 0), (3, 1), (1, 3), (2, 2))[stage + 1]]
         out = []
         for j in (0, 1):
             for way in (0, 1):
                 yy = y if not inbound else ((y + 3) % 4 if way == 0 else (y + 1) % 4)
-                c = chunk(yy, zz[j], j, first, rows)
+                c = chunk(yy, zz[j], h, j, first, rows)
                 n = j * 2 + way
                 out.append(rc(c, c, y_s.at[n, i], y_r.at[n, i], d_up if way == 0 else d_down))
         return out
 
     def y_forward(i, inbound):
-        stage, first, rows = UNITS[i]
+        h, stage, first, rows = UNITS[i]
         zz = [(zh + n) % 4 for n in ((0, 0), (3, 1), (1, 3), (2, 2))[stage + 1]]
         out = []
         for j in (0, 1):
             away = 1 + inbound
             yy = (y + 4 - away) % 4 if j == 0 else (y + away) % 4
-            c = chunk(yy, zz[j], j, first, rows)
+            c = chunk(yy, zz[j], h, j, first, rows)
             out.append(rc(c, c, y_s.at[4 + j, i], y_r.at[4 + j, i], d_up if j == 0 else d_down))
         return out
 
@@ -168,21 +173,64 @@
         b = e.at[pl.ds(((zl + 4 - r) % 4) * 4 + cc * 2, 2)]
         return rc(b, b, ec_s.at[r], ec_r.at[r], d_sib)
 
-    def add_block(yy, zz):
+    def add_block(h, yy, zz):
         d = yy * 4 + zz
         rows = e[d]
         for j in (0, 1):
-            acc[j] = acc[j] + dot(rows, w[d, j], NN)
-
-    def own(k):
-        add_block((y + k) % 4, zh)
-
-    def neighbours(k):
-        add_block((y + k) % 4, (zh + 1) % 4)
-        add_block((y + k) % 4, (zh + 3) % 4)
-
-    def far(k):
-        add_block((y + k) % 4, (zh + 2) % 4)
+            acc[h, j] = acc[h, j] + dot(rows, w[d, h, j], NN)
+
+    def add_own(h):
+        loop(0, 4, lambda k: add_block(h, (y + k) % 4, zh))
+
+    def add_near(h):
+        def step(k):
+            add_block(h, (y + k) % 4, (zh + 1) % 4)
+            add_block(h, (y + k) % 4, (zh + 3) % 4)
+
+        loop(0, 4, step)
+
+    def add_far(h):
+        loop(0, 4, lambda k: add_block(h, (y + k) % 4, (zh + 2) % 4))
+
+    def attend(h):
+        scale = HD ** -0.5
+        shape = (256, 256)
+        visible = lax.broadcasted_iota(jnp.int32, shape, 1) < enc_len[0]
+        live = lax.broadcasted_iota(jnp.int32, shape, 0) < dec_len[0]
+        cols = slice(h * HD, (h + 1) * HD)
+        q = q_v[:, cols]
+        key, value = acc[h, 0].astype(BF), acc[h, 1].astype(BF)
+        masked = jnp.where(live, dc_v[:, cols].astype(F32), 0.0)
+        masked16 = masked.astype(BF)
+        scores = jnp.where(visible, dot(q, key, NT) * scale, NEG)
+        powers = jnp.exp(scores - jnp.max(scores, axis=1, keepdims=True))
+        attention = powers / jnp.sum(powers, axis=1, keepdims=True)
+        rounded = attention.astype(BF)
+        context = dot(rounded, value, NN).astype(BF)
+        weights = dot(masked16, value, NT)
+        inner = jnp.sum(masked * context.astype(F32), axis=1, keepdims=True)
+        g = (attention * (weights - inner) * scale).astype(BF)
+        grads[h, 0] = dot(g, q, TN).astype(BF)
+        grads[h, 1] = dot(rounded, masked16, TN).astype(BF)
+        ctx_ref[0, :, cols] = context
+        gq_ref[0, :, cols] = dot(g, key, NN).astype(BF)
+
+    def place(k):
+        return (zl + 1 + k) % 4
+
+    def enc_term(h, k, cc, half):
+        d = place(k) * 4 + cc * 2 + half
+        return dot(grads[h, 0], w[d, h, 0], NT) + dot(grads[h, 1], w[d, h, 1], NT)
+
+    def early_terms(other):
+        def step(k):
+            for half in (0, 1):
+                if other:
+                    away[k, half] = enc_term(0, k, 1 - core, half)
+                else:
+                    part[k, half] = enc_term(0, k, core, half)
+
+        loop(0, 4, step)
 
     def enc_stage(n):
         if n == 0:
@@ -230,52 +278,37 @@
         start(y_direct(NO + t, 0))
         sent(z_copy(t, 0))
         if t + DEPTH < NZ:
+            for dev in d_line[1:]:
+                pl.semaphore_signal(cred.at[t], inc=1, device_id=dev, device_id_type=pl.DeviceIdType.MESH)
+            pl.semaphore_wait(cred.at[t], 3)
             start(z_copy(t + DEPTH, 0))
         y_until(min(NO + t - LAG, (NU * (t + 1)) // NZ))
-        enc_stage(t - 1)
-        if t == 9:
+        enc_stage(ENC.index(t) if t in ENC else -1)
+        if t == NZ0 - 1:
             late_until(NO)
-            loop(0, 4, own)
-    near = NO + len(FIRST) + len(SECOND)
+            add_own(0)
+            add_own(1)
+        if t == NZ0 + 1:
+            late_until(NO + CUT_NEAR)
+            add_near(0)
+        if t == NZ0 + 2:
+            late_until(NO + NZ0)
+            add_far(0)
+        if t == NZ0 + 4:
+            for copy in loads[6:]:
+                copy.wait()
+            attend(0)
+        if t == NZ0 + 6:
+            early_terms(True)
+        if t == NZ0 + 8:
+            early_terms(False)
     y_until(NU - 1)
-    late_until(near)
-    loop(0, 4, neighbours)
+    late_until(NU - len(HEAD1[2]))
+    add_near(1)
     y_until(NU)
     late_until(NU)
-    loop(0, 4, far)
-
-    for copy in loads[4:]:
-        copy.wait()
-    scale = HD ** -0.5
-    kv[...] = acc[...].astype(BF)
-    shape = (256, 256)
-    visible = lax.broadcasted_iota(jnp.int32, shape, 1) < enc_len[0]
-    live = lax.broadcasted_iota(jnp.int32, shape, 0) < dec_len[0]
-    for h in (0, 1):
-        cols = slice(h * HD, (h + 1) * HD)
-        q = q_v[:, cols]
-        key, value = kv[0, :, cols], kv[1, :, cols]
-        masked = jnp.where(live, dc_v[:, cols].astype(F32), 0.0)
-        masked16 = masked.astype(BF)
-        scores = jnp.where(visible, dot(q, key, NT) * scale, NEG)
-        powers = jnp.exp(scores - jnp.max(scores, axis=1, keepdims=True))
-        attention = powers / jnp.sum(powers, axis=1, keepdims=True)
-        rounded = attention.astype(BF)
-        context = dot(rounded, value, NN).astype(BF)
-        ctx_ref[0, :, cols] = context
-        weights = dot(masked16, value, NT)
-        inner = jnp.sum(masked * context.astype(F32), axis=1, keepdims=True)
-        g = (attention * (weights - inner) * scale).astype(BF)
-        gq_ref[0, :, cols] = dot(g, key, NN).astype(BF)
-        grads[0, :, cols] = dot(g, q, TN).astype(BF)
-        grads[1, :, cols] = dot(rounded, masked16, TN).astype(BF)
-
-    def place(k):
-        return (zl + 1 + k) % 4
-
-    def enc_term(k, cc, half):
-        d = place(k) * 4 + cc * 2 + half
-        return dot(grads[0], w[d, 0], NT) + dot(grads[1], w[d, 1], NT)
+    add_far(1)
+    attend(1)
 
     def c_copy(k):
         return rc(s0.at[k], r0.at[k], c_s.at[k], c_r.at[k], d_sib)
@@ -300,12 +333,12 @@
 
     def to_sibling(k):
         for half in (0, 1):
-            s0[k, half] = enc_term(k, 1 - core, half).astype(BF)
+            s0[k, half] = (away[k, half] + enc_term(1, k, 1 - core, half)).astype(BF)
         c_copy(k).start()
 
     def mine(k):
         for half in (0, 1):
-            part[k, half] = enc_term(k, core, half)
+            part[k, half] = part[k, half] + enc_term(1, k, core, half)
         c_copy(k).wait_recv()
         part[k] = part[k] + r0[k].astype(F32)
         for way in (0, 1):
@@ -315,9 +348,9 @@
     def second(k):
         received(x1_copy(k))
         for way in (0, 1):
-            away = quarter(1 + 2 * way)
+            other = quarter(1 + 2 * way)
             for half in (0, 1):
-                term = part[k, half, away, :]
+                term = part[k, half, other, :]
                 if half == way:
                     term = term + x1r[k, way].astype(F32)
                 x2s[k, way, half] = term.astype(BF)
@@ -328,8 +361,9 @@
         total = part[k, :, quarter(0), :] + x2r[k, 0].astype(F32) + x2r[k, 1].astype(F32)
         part[k, :, quarter(0), :] = total
 
-    loop(0, 4, to_sibling)
-    loop(0, 4, mine)
+    to_sibling(0)
+    loop(0, 3, lambda k: (to_sibling(k + 1), mine(k)))
+    mine(3)
     loop(0, 4, second)
     for k in range(3):
         third(k)
@@ -379,11 +413,11 @@
         in_specs=[smem, smem] + [hbm] * 5,
         out_specs=(vmem, vmem, vmem),
         scratch_shapes=[
-            pltpu.VMEM((16, 2, 256, 512), BF),
+            pltpu.VMEM((16, 2, 2, 256, 256), BF),
             pltpu.VMEM((16, 256, 256), BF),
-            pltpu.VMEM((2, 256, 512), F32),
-            pltpu.VMEM((2, 256, 512), BF),
-            pltpu.VMEM((2, 256, 512), BF),
+            pltpu.VMEM((2, 2, 256, 256), F32),
+            pltpu.VMEM((2, 2, 256, 256), BF),
+            pltpu.VMEM((4, 2, 256, 256), F32),
             pltpu.VMEM((4, 2, 256, 256), BF),
             pltpu.VMEM((4, 2, 256, 256), BF),
             pltpu.VMEM((4, 2, 256, 256), F32),
@@ -401,12 +435,13 @@
             dma((4,)), dma((4,)),
             dma((4, 2)), dma((4, 2)),
             dma((4, 2)), dma((4, 2)),
-            dma((3,)), dma((3,)), dma((6,)),
+            dma((3,)), dma((3,)), dma((8,)),
             pltpu.VMEM((256, 512), BF),
             pltpu.VMEM((256, 512), BF),
+            pltpu.SemaphoreType.REGULAR((NZ,)),
         ],
         compiler_params=pltpu.CompilerParams(
-            collective_id=0, has_side_effects=True, vmem_limit_bytes=64 * 1024 * 1024
+            collective_id=0, has_side_effects=True, vmem_limit_bytes=55836672
         ),
         cost_estimate=pl.CostEstimate(flops=5 * 10**9, bytes_accessed=2 * 10**6, transcendentals=131072),
         name="fused",

time: 142 us -> 130 us (0.915)
  Pallas kernels: 137 us -> 125 us
    pallas_call x1, Pallas kernels: 137 us -> 125 us  [body(): pl.pallas_call(kernel, out_shape=(jax.ShapeDtypeStruct((1, 256, 512), BF)...]
    unnamed x7 -> x5, local copies, waits for them, and re-layouts: 3.37 us -> 2.89 us
where the time goes in v3:
time: 130 us
  Pallas kernels  125 us (96%)
  local copies, waits for them, and re-layouts  2.89 us (2%)
  between operations  1.94 us (1%)
    pallas_call x1, Pallas kernels, body(): pl.pallas_call(kernel, out_shape=(jax.ShapeDtypeStruct((1, 256, 512), BF)...  125 us
    unnamed x5, local copies, waits for them, and re-layouts  2.89 us

profile of v3, /device:TPU:24, one launch (start us, length us, event | category | flops | bytes accessed | tf_op | source)
XLA Modules:
  0.0 129.8 jit_solution(6770377321467658936)
XLA Ops:
  1.9 0.0 copy-start
  1.9 0.8 copy-done
  2.8 124.9 %fused.1 = (bf16[1,256,512]{2,1,0:T(8,128)(2,1)S(1)}, bf16[1,256,512]{2,1,0:T(8,128)(2,1)S(1)}, f32[64,512]{1,0:T(8,128)S(1)}) custom-call(s32[1]{0:T(128)S(6)} %copy.13.enc_len, s32[1]{0:T(128)S(6)} %copy.14.dec_len, bf16[64,512]{1,0:T(8,128)(2,1)S(1)} %copy-done, bf16[1,256,512]{2,1,0:T(8,128)(2,1)} %q_ref.1, bf16[1,256,512]{2,1,0:T(8,128)(2,1)} %wk_ref.1, ...), custom_call_target="tpu_custom_call" | custom-call | flops 5000000000 | bytes 2000000 | tf_op jit(solution)/shard_map/fused/pallas_call | solution.py:406
  127.7 0.7 copy.15
  128.4 0.7 copy.16
  129.1 0.7 copy.17
Async XLA Ops:
  1.9 0.8 copy-start

commit v4 on v3

--- a/solution.py
+++ b/solution.py
@@ -306,8 +306,10 @@
     late_until(NU - len(HEAD1[2]))
     add_near(1)
     y_until(NU)
+    for k in (0, 1, 3):
+        add_block(1, (y + k) % 4, (zh + 2) % 4)
     late_until(NU)
-    add_far(1)
+    add_block(1, (y + 2) % 4, (zh + 2) % 4)
     attend(1)
 
     def c_copy(k):

time: 130 us -> 129 us (level)
  no operation moved by 1% of the time
where the time goes in v4:
time: 129 us
  Pallas kernels  124 us (96%)
  local copies, waits for them, and re-layouts  2.89 us (2%)
  between operations  1.94 us (2%)
    pallas_call x1, Pallas kernels, body(): pl.pallas_call(kernel, out_shape=(jax.ShapeDtypeStruct((1, 256, 512), BF)...  124 us
    unnamed x5, local copies, waits for them, and re-layouts  2.89 us

profile of v4, /device:TPU:24, one launch (start us, length us, event | category | flops | bytes accessed | tf_op | source)
XLA Modules:
  0.0 129.0 jit_solution(5366286125308074356)
XLA Ops:
  1.9 0.0 copy-start
  1.9 0.8 copy-done
  2.8 124.2 %fused.1 = (bf16[1,256,512]{2,1,0:T(8,128)(2,1)S(1)}, bf16[1,256,512]{2,1,0:T(8,128)(2,1)S(1)}, f32[64,512]{1,0:T(8,128)S(1)}) custom-call(s32[1]{0:T(128)S(6)} %copy.13.enc_len, s32[1]{0:T(128)S(6)} %copy.14.dec_len, bf16[64,512]{1,0:T(8,128)(2,1)S(1)} %copy-done, bf16[1,256,512]{2,1,0:T(8,128)(2,1)} %q_ref.1, bf16[1,256,512]{2,1,0:T(8,128)(2,1)} %wk_ref.1, ...), custom_call_target="tpu_custom_call" | custom-call | flops 5000000000 | bytes 2000000 | tf_op jit(solution)/shard_map/fused/pallas_call | solution.py:408
  127.0 0.7 copy.15
  127.7 0.7 copy.16
  128.4 0.7 copy.17
Async XLA Ops:
  1.9 0.8 copy-start
